TPU v7x, 32 devices: a whole 2x2x4 slice. The times are simulated.
32 devices in a mesh: rep: 2 (over y), pool: 16 (over z, x, core).
Axes of the slice: x: 2, y: 2, z: 4, core: 2. Of those that a mesh axis runs over, the one named last changes fastest.
Arguments:
- tokens: bfloat16 [4096, 8192], P(('rep', 'pool')), parts along dimension 0, may hold values from -6 to 6
- key_projection_weight: bfloat16 [8192, 1024], P('pool'), may hold values from -0.0625 to 0.0625
- adapter_down_factors: bfloat16 [32, 8192, 64], P(('rep', 'pool')), parts along dimension 0, may hold values from -0.0625 to 0.0625
- adapter_up_factors: bfloat16 [32, 64, 1024], P(('rep', 'pool')), parts along dimension 0, may hold values from -0.75 to 0.75
- request_adapter_index: int32 [4096, 1], P(('rep', 'pool')), parts along dimension 0, may hold values from 0 to 15; in each aligned block of 128 rows (0 to 127, 128 to 255, ...) at most 16 rows name the same one
Outputs:
- queries: bfloat16 [4096, 1024], P(('rep', 'pool')), parts along dimension 0
There are 2 independent parts, one for each index of `rep`. A program takes and returns all parts, laid end to end along the dimension named above; an argument that names none is the same for every part. Nothing has to cross between parts.
Inputs may be any that keep to these rules, and one draw needn't show every extreme that they name: `request_adapter_index`: in each aligned block of 128 rows (the rows of one index of pool) no adapter is named by more than 16 rows, a bound that some block reaches.
All inputs are finite; a program needn't handle non-finite values.
Results may differ from a plain program's by a relative error of at most 0.0055.
Values may be sent and summed in bfloat16 or wider, within the bound.
A program may use at most 128 MiB of HBM per device.

v0:
```python
import jax
import jax.numpy as jnp
from jax import lax
from jax.sharding import PartitionSpec as P


def local(
    tokens, key_projection_weight, adapter_down_factors, adapter_up_factors, request_adapter_index
):
    row_count = tokens.shape[0]
    width = tokens.shape[1]
    devices = lax.axis_size("pool")
    rows_by_device = adapter_down_factors.shape[0]
    out_width = key_projection_weight.shape[1]
    per_adapter = max(2, 2 * row_count // (rows_by_device * devices))
    capacity = rows_by_device * per_adapter
    adapter_col = request_adapter_index[:, 0]
    same = adapter_col[:, None] == adapter_col[None, :]
    positions = jnp.arange(row_count, dtype=jnp.int32)
    earlier = positions[None, :] < positions[:, None]
    rank_within = jnp.sum((same & earlier).astype(jnp.int32), axis=1)
    slot_index = adapter_col * per_adapter + rank_within
    base = jnp.dot(
        tokens,
        lax.all_gather(key_projection_weight, "pool", axis=0, tiled=True),
        preferred_element_type=jnp.float32,
    )
    outgoing = jnp.zeros((devices * capacity, width), jnp.bfloat16).at[slot_index].set(tokens)
    outgoing = outgoing.reshape(devices, capacity, width)
    received_rows = lax.all_to_all(outgoing, "pool", split_axis=0, concat_axis=0, tiled=True)
    received_rows = received_rows.reshape(devices, rows_by_device, per_adapter, width)
    rank_reduced = jnp.einsum(
        "qhey,hyt->qhet", received_rows, adapter_down_factors, preferred_element_type=jnp.float32
    ).astype(jnp.bfloat16)
    expanded = jnp.einsum(
        "zydk,ykj->zydj", rank_reduced, adapter_up_factors, preferred_element_type=jnp.float32
    ).astype(jnp.bfloat16)
    returned = lax.all_to_all(
        expanded.reshape(devices, capacity, out_width),
        "pool",
        split_axis=0,
        concat_axis=0,
        tiled=True,
    )
    delta = returned.reshape(devices * capacity, out_width)[slot_index]
    return (base + 2.0 * delta.astype(jnp.float32)).astype(jnp.bfloat16)


def solution(mesh):
    in_specs = (
        P(("rep", "pool"), None),
        P("pool", None),
        P(("rep", "pool"), None, None),
        P(("rep", "pool"), None, None),
        P(("rep", "pool"), None),
    )
    out_specs = P(("rep", "pool"), None)
    return jax.shard_map(local, mesh=mesh, in_specs=in_specs, out_specs=out_specs, check_vma=False)
```

profile of v0, /device:TPU:0, one launch (start us, length us, event | category | flops | bytes accessed | tf_op | source)
XLA Modules:
  0.0 248.6 jit_solution(15033605059063231599)
XLA Ops:
  6.5 0.0 copy-start
  6.5 0.0 all-gather.2.cloned.1.call-start
  6.5 0.7 all-gather.2.cloned.1.call-update
  7.3 0.9 convert_reduce_fusion
  8.2 0.7 fusion.7
  8.8 7.0 %scatter_custom_fusion = bf16[256,8192]{1,0:T(8,128)(2,1)} fusion(s32[128]{0:T(128)S(1)} %fusion.7, bf16[128,8192]{1,0:T(8,128)(2,1)} %param.5, bf16[]{:T(256)} %constant.5.clone.1), kind=kCustom, calls=%fused_computation.2 | custom fusion | bytes 4194816 | tf_op jit(solution)/shard_map/scatter | solution.py:28
  15.8 0.0 copy-start.1
  15.9 189.8 %all_to_all.10 = bf16[16,16,8192]{2,1,0:T(8,128)(2,1)} all-to-all(bf16[16,16,8192]{2,1,0:T(8,128)(2,1)} %bitcast.21), channel_id=1, replica_groups=mesh['rep'=2,'pool'=16] {'pool'}, dimensions={0} | all-to-all | bytes 8388608 | tf_op jit(solution)/shard_map/all_to_all | solution.py:30
  205.6 0.0 copy-done
  205.6 0.0 copy-done.1
  205.6 4.9 %convolution_convert_fusion = bf16[16,16,1024]{2,1,0:T(8,128)(2,1)} fusion(bf16[16,16,8192]{2,1,0:T(8,128)(2,1)} %all_to_all.10, bf16[1,8192,64]{1,2,0:T(8,128)(2,1)S(1)} %copy-done, bf16[1,64,1024]{2,1,0:T(8,128)(2,1)S(1)} %copy-done.1), kind=kOutput, calls=%fused_computation.4 | convolution fusion | flops 302268416 | bytes 5898240 | tf_op jit(solution)/shard_map/zydk,ykj->zydj/dot_general | solution.py:35
  210.6 6.4 %all-to-all-start.1 = ((bf16[16,16,1024]{2,1,0:T(8,128)(2,1)}), bf16[16,16,1024]{2,1,0:T(8,128)(2,1)S(1)}, u32[]{:S(2)}, u32[]{:S(2)}) async-start(bf16[16,16,1024]{2,1,0:T(8,128)(2,1)} %convolution_convert_fusion), calls=%async_computation.1 | async-start | bytes 1048576 | tf_op jit(solution)/shard_map/all_to_all | solution.py:38
  217.0 14.5 %all-to-all-done.1 = bf16[16,16,1024]{2,1,0:T(8,128)(2,1)S(1)} async-done(((bf16[16,16,1024]{2,1,0:T(8,128)(2,1)}), bf16[16,16,1024]{2,1,0:T(8,128)(2,1)S(1)}, u32[]{:S(2)}, u32[]{:S(2)}) %all-to-all-start.1) | async-done | bytes 524320 | tf_op jit(solution)/shard_map/all_to_all | solution.py:38
  231.4 0.9 gather_fusion
  232.3 0.0 all-gather.2.cloned.1.call-done
  232.3 9.5 %fusion.2 = bf16[128,1024]{1,0:T(8,128)(2,1)} fusion(bf16[128,8192]{1,0:T(8,128)(2,1)} %param.5, bf16[8192,1024]{1,0:T(8,128)(2,1)} %all-gather.2.cloned.1.call-done, bf16[128,1024]{1,0:T(8,128)(2,1)S(1)} %gather_fusion), kind=kOutput, calls=%fused_computation.6 | convolution fusion | flops 2148007936 | bytes 19398656 | tf_op jit(solution)/shard_map/dot_general | solution.py:23
  (1 shorter events, 0.0 us)
Async XLA Ops:
  6.5 199.1 %copy-start = (bf16[1,8192,64]{1,2,0:T(8,128)(2,1)S(1)}, bf16[1,8192,64]{1,2,0:T(8,128)(2,1)}, u32[]{:S(2)}) copy-start(bf16[1,8192,64]{1,2,0:T(8,128)(2,1)} %param.7) | copy-start | bytes 3145732
  6.5 225.8 %all-gather.2.cloned.1.call-start = ((), (), s32[]{:S(2)}) async-start(), calls=%async_computation.2 | async-start | bytes 17825792 | tf_op jit(solution)/shard_map/all_gather | solution.py:25
  15.8 189.8 %copy-start.1 = (bf16[1,64,1024]{2,1,0:T(8,128)(2,1)S(1)}, bf16[1,64,1024]{2,1,0:T(8,128)(2,1)}, u32[]{:S(2)}) copy-start(bf16[1,64,1024]{2,1,0:T(8,128)(2,1)} %param.8) | copy-start | bytes 393220
  210.6 20.9 %all-to-all-start.1 = ((bf16[16,16,1024]{2,1,0:T(8,128)(2,1)}), bf16[16,16,1024]{2,1,0:T(8,128)(2,1)S(1)}, u32[]{:S(2)}, u32[]{:S(2)}) async-start(bf16[16,16,1024]{2,1,0:T(8,128)(2,1)} %convolution_convert_fusion), calls=%async_computation.1 | async-start | bytes 1048576 | tf_op jit(solution)/shard_map/all_to_all | solution.py:38
Sparse Core Ops, SparseCore 0:
  9.5 209.0 all-gather.1
where the time goes:
time: 249 us
  blocking collectives  190 us (76%)
  waiting for transfers between devices  15.2 us (6%)
  matrix products  14.4 us (6%)
  between operations  13.4 us (5%)
  local copies, waits for them, and re-layouts  7.89 us (3%)
  starting transfers between devices  6.38 us (3%)
    all_to_all x1, blocking collectives, local(): lax.all_to_all(outgoing, 'pool', split_axis=0, concat_axis=0, tiled=True)  190 us
    all_to_all x1, waiting for transfers between devices, local(): lax.all_to_all(expanded.reshape(devices, capacity, out_width), 'pool', sp...  14.5 us
    dot_general x1, matrix products, local(): jnp.dot(tokens, lax.all_gather(key_projection_weight, 'pool', axis=0, til...  9.45 us
    scatter x1, local copies, waits for them, and re-layouts, local(): jnp.zeros((devices * capacity, width), jnp.bfloat16).at[slot_index]  7.02 us
    all_to_all x1, starting transfers between devices, local(): lax.all_to_all(expanded.reshape(devices, capacity, out_width), 'pool', sp...  6.38 us
  transfers between devices with their start and end apart: 2, of which 1 were waited for; matrix products, arithmetic and copies ran while one was open for 6% of the time, Pallas kernels for 0%

commit v1 on v0

--- a/solution.py
+++ b/solution.py
@@ -1,10 +1,270 @@
+import functools
+
 import jax
 import jax.numpy as jnp
 from jax import lax
+from jax.experimental import pallas as pl
+from jax.experimental.pallas import tpu as pltpu
 from jax.sharding import PartitionSpec as P
 
-
-def local(
+HALVES = 2
+LANES = 128
+MESH = pl.DeviceIdType.MESH
+
+
+def kernel(
+    group, reps, parts,
+    x_hbm, w_hbm, a_ref, b_hbm, id_ref, out_ref,
+    apack, xr, ar, wf, bp, idr, idb, acc0, acc1, sp, srecv, s2, s2m, cpart, crecv,
+    x_send, x_recv, a_send, a_recv, w_send, w_recv, f_send, f_recv, b_send, b_recv,
+    i_send, i_recv, s_send, s_recv, t_send, t_recv, c_send, c_recv, local_sem,
+):
+    rep = lax.axis_index("rep")
+    pool = lax.axis_index("pool")
+    half, e = pool // group, pool % group
+    rows, out_width = out_ref.shape
+    depth = w_hbm.shape[0]
+    low = group * depth
+    rank = b_hbm.shape[0]
+    devices = group * HALVES
+    part = out_width // parts
+    partner = (pool + group) % devices
+
+    def peer(k):
+        return half * group + (e + k) % group
+
+    def row_at(i):
+        return pl.ds(pl.multiple_of(i * rows, rows), rows)
+
+    def col_at(i, size):
+        return pl.ds(pl.multiple_of(i * size, size), size)
+
+    def remote(src, dst, send, recv, device):
+        return pltpu.make_async_remote_copy(
+            src_ref=src, dst_ref=dst, send_sem=send, recv_sem=recv,
+            device_id=device, device_id_type=MESH,
+        )
+
+    barrier = pltpu.get_barrier_semaphore()
+    for k in range(1, devices):
+        pl.semaphore_signal(
+            barrier, inc=1, device_id={"pool": (pool + k) % devices}, device_id_type=MESH
+        )
+    for k in range(1, reps):
+        pl.semaphore_signal(
+            barrier, inc=1, device_id={"rep": (rep + k) % reps}, device_id_type=MESH
+        )
+
+    own = [
+        pltpu.make_async_copy(
+            x_hbm.at[:, pl.ds(pl.multiple_of(b * low + e * depth, depth), depth)],
+            xr.at[b, row_at(e)], local_sem.at[b],
+        )
+        for b in range(HALVES)
+    ]
+    own.append(pltpu.make_async_copy(w_hbm, wf.at[half], local_sem.at[2]))
+    own_b = pl.ds(pl.multiple_of(half * rank, rank), rank)
+    own.append(pltpu.make_async_copy(b_hbm, bp.at[own_b], local_sem.at[3]))
+    for copy in own:
+        copy.start()
+
+    @pl.loop(0, group)
+    def _(i):
+        at = pl.ds(pl.multiple_of(i * depth, depth), depth)
+        up = pl.ds(pl.multiple_of(low + i * depth, depth), depth)
+        apack[at] = jnp.concatenate([a_ref[at], a_ref[up]], axis=1)
+
+    ar[:, col_at(pool, LANES)] = apack[pl.ds(pl.multiple_of(e * depth, depth), depth)]
+    idr[e] = id_ref[...]
+    pl.semaphore_wait(barrier, devices - 1 + reps - 1)
+
+    sends, arrivals = [], []
+
+    def launch(copy, wanted=True):
+        copy.start()
+        sends.append(copy)
+        if wanted:
+            arrivals.append(copy)
+        return copy
+
+    def send_a(n, device):
+        to = device % group
+        launch(remote(
+            apack.at[pl.ds(pl.multiple_of(to * depth, depth), depth)],
+            ar.at[:, col_at(pool, LANES)], a_send.at[n], a_recv.at[n], {"pool": device},
+        ))
+
+    for k in range(1, group):
+        launch(remote(id_ref, idr.at[e], i_send.at[k], i_recv.at[k], {"pool": peer(k)}))
+    for k in range(1, group):
+        for b in range(HALVES):
+            to = (e + k) % group
+            launch(remote(
+                x_hbm.at[:, pl.ds(pl.multiple_of(b * low + to * depth, depth), depth)],
+                xr.at[b, row_at(e)], x_send.at[b, k], x_recv.at[b, k], {"pool": peer(k)},
+            ))
+        send_a(k, peer(k))
+        send_a(group + k, (1 - half) * group + (e + k) % group)
+    send_a(group, partner)
+    share = parts // reps
+    w_copies = []
+    for n in range(share):
+        at = col_at(n * reps + rep, part)
+        w_copies.append(launch(remote(
+            w_hbm.at[:, at], wf.at[half, :, at], w_send.at[n], w_recv.at[n], {"pool": partner},
+        ), False))
+    b_copy = launch(remote(b_hbm, bp.at[own_b], b_send, b_recv, {"pool": partner}), False)
+
+    for copy in arrivals:
+        copy.wait_recv()
+    for copy in own:
+        copy.wait()
+
+    lane = lax.broadcasted_iota(jnp.int32, (rows, LANES), 1)
+    eye = lane == lax.broadcasted_iota(jnp.int32, (rows, LANES), 0)
+
+    @pl.loop(0, group)
+    def _(i):
+        line = jnp.broadcast_to(idr[i][0:1, :], (rows, LANES))
+        column = jnp.sum(jnp.where(eye, line, 0.0), axis=1, keepdims=True)
+        idb[row_at(i)] = jnp.broadcast_to(column, (rows, LANES))
+
+    acc0[...] = jnp.zeros_like(acc0)
+    acc1[...] = jnp.zeros_like(acc1)
+
+    @pl.loop(0, devices // 2)
+    def _(j):
+        at = col_at(j, 2 * LANES)
+        ids = idb[...]
+        first = (2 * j).astype(jnp.float32)
+        for b, acc in ((0, acc0), (1, acc1)):
+            t = jnp.dot(xr[b], ar[:, at], preferred_element_type=jnp.float32)
+            acc[...] = jnp.where(
+                ids == first, t[:, :LANES],
+                jnp.where(ids == first + 1.0, t[:, LANES:], acc[...]),
+            )
+
+    wide = lax.broadcasted_iota(jnp.int32, acc0.shape, 1)
+    sp[...] = jnp.where(wide < rank, acc0[...], acc1[...]).astype(jnp.bfloat16)
+    s_copies = []
+    for k in range(1, group):
+        to = (e + k) % group
+        s_copies.append(launch(remote(
+            sp.at[row_at(to)], srecv.at[k], s_send.at[k], s_recv.at[k], {"pool": peer(k)},
+        ), False))
+    other = (rep + 1) % reps
+    f_copies = []
+    for n in range(share):
+        w_copies[n].wait_recv()
+        at = col_at(n * reps + rep, part)
+        piece = wf.at[1 - half, :, at]
+        f_copies.append(launch(remote(
+            piece, piece, f_send.at[n], f_recv.at[n], {"rep": other},
+        ), False))
+    total = sp[row_at(e)].astype(jnp.float32)
+    for k in range(1, group):
+        s_copies[k - 1].wait_recv()
+        total += srecv[k].astype(jnp.float32)
+    total = total + pltpu.roll(total, rank, 1)
+    upper = idb[row_at(e)] >= float(group)
+    s2[row_at(e)] = jnp.where(upper == (lane >= rank), total, 0.0).astype(jnp.bfloat16)
+    t_copies = []
+    for k in range(1, group):
+        t_copies.append(launch(remote(
+            s2.at[row_at(e)], s2.at[row_at(e)], t_send.at[k], t_recv.at[k], {"pool": peer(k)},
+        ), False))
+    for copy in t_copies:
+        copy.wait_recv()
+    b_copy.wait_recv()
+    mine = e.astype(jnp.float32)
+    ids = idb[...]
+    here = (ids == mine) | (ids == mine + float(group))
+    s2m[...] = jnp.where(here, 2.0 * s2[...].astype(jnp.float32), 0.0).astype(jnp.bfloat16)
+
+    for copy in f_copies:
+        copy.wait_recv()
+    c_copies = []
+    for j in range(parts):
+        at = pl.ds(j * part, part)
+        value = jnp.dot(s2m[...], bp[:, at], preferred_element_type=jnp.float32)
+        for b in range(HALVES):
+            value += jnp.dot(xr[b], wf[b, :, at], preferred_element_type=jnp.float32)
+        cpart[:, at] = value.astype(jnp.bfloat16)
+        for k in range(1, group):
+            to = (e + k) % group
+            c_copies.append(launch(remote(
+                cpart.at[row_at(to), at], crecv.at[k, :, at],
+                c_send.at[j, k], c_recv.at[j, k], {"pool": peer(k)},
+            ), False))
+    for j in range(parts):
+        at = pl.ds(j * part, part)
+        value = cpart[row_at(e), at].astype(jnp.float32)
+        for k in range(1, group):
+            c_copies[j * (group - 1) + k - 1].wait_recv()
+            value += crecv[k, :, at].astype(jnp.float32)
+        out_ref[:, at] = value.astype(jnp.bfloat16)
+    for copy in sends:
+        copy.wait_send()
+
+
+def split_depth(
+    tokens, key_projection_weight, adapter_down_factors, adapter_up_factors, request_adapter_index
+):
+    rows = tokens.shape[0]
+    depth, out_width = key_projection_weight.shape
+    rank = adapter_down_factors.shape[2]
+    devices = lax.axis_size("pool")
+    reps = lax.axis_size("rep")
+    group = devices // HALVES
+    parts = 2 * reps
+    everyone = group * rows
+    ids = jnp.broadcast_to(
+        request_adapter_index.astype(jnp.float32).reshape(1, rows), (8, rows)
+    )
+    bf16, f32 = jnp.bfloat16, jnp.float32
+    dma = pltpu.SemaphoreType.DMA
+    hbm, vmem = pl.BlockSpec(memory_space=pl.ANY), pl.BlockSpec(memory_space=pltpu.VMEM)
+    return pl.pallas_call(
+        functools.partial(kernel, group, reps, parts),
+        out_shape=jax.ShapeDtypeStruct((rows, out_width), bf16),
+        in_specs=[hbm, hbm, vmem, hbm, vmem],
+        out_specs=vmem,
+        scratch_shapes=[
+            pltpu.VMEM((group * depth, LANES), bf16),
+            pltpu.VMEM((HALVES, everyone, depth), bf16),
+            pltpu.VMEM((depth, devices * LANES), bf16),
+            pltpu.VMEM((HALVES, depth, out_width), bf16),
+            pltpu.VMEM((HALVES * rank, out_width), bf16),
+            pltpu.VMEM((group, 8, rows), f32),
+            pltpu.VMEM((everyone, LANES), f32),
+            pltpu.VMEM((everyone, LANES), f32),
+            pltpu.VMEM((everyone, LANES), f32),
+            pltpu.VMEM((everyone, LANES), bf16),
+            pltpu.VMEM((group, rows, LANES), bf16),
+            pltpu.VMEM((everyone, LANES), bf16),
+            pltpu.VMEM((everyone, LANES), bf16),
+            pltpu.VMEM((everyone, out_width), bf16),
+            pltpu.VMEM((group, rows, out_width), bf16),
+            dma((HALVES, group)), dma((HALVES, group)),
+            dma((devices,)), dma((devices,)),
+            dma((parts,)), dma((parts,)),
+            dma((parts,)), dma((parts,)),
+            dma, dma,
+            dma((group,)), dma((group,)),
+            dma((group,)), dma((group,)),
+            dma((group,)), dma((group,)),
+            dma((parts, group)), dma((parts, group)),
+            dma((4,)),
+        ],
+        compiler_params=pltpu.CompilerParams(
+            collective_id=0, has_side_effects=True, vmem_limit_bytes=48 << 20
+        ),
+    )(
+        tokens, key_projection_weight, adapter_down_factors[0], adapter_up_factors[0], ids
+    )
+
+
+def route_rows(
     tokens, key_projection_weight, adapter_down_factors, adapter_up_factors, request_adapter_index
 ):
     row_count = tokens.shape[0]
@@ -46,6 +306,24 @@
     return (base + 2.0 * delta.astype(jnp.float32)).astype(jnp.bfloat16)
 
 
+def local(
+    tokens, key_projection_weight, adapter_down_factors, adapter_up_factors, request_adapter_index
+):
+    fits = (
+        key_projection_weight.shape[0] % LANES == 0
+        and tokens.shape[0] == LANES
+        and adapter_down_factors.shape[0] == 1
+        and HALVES * adapter_down_factors.shape[2] == LANES
+        and lax.axis_size("pool") % HALVES == 0
+        and lax.axis_size("rep") == 2
+    )
+    plan = split_depth if fits else route_rows
+    return plan(
+        tokens, key_projection_weight, adapter_down_factors, adapter_up_factors,
+        request_adapter_index,
+    )
+
+
 def solution(mesh):
     in_specs = (
         P(("rep", "pool"), None),

time: 249 us -> 125 us (0.50)
  blocking collectives: 190 us -> 0 us
  Pallas kernels: 0 us -> 119 us
  waiting for transfers between devices: 15.2 us -> 0 us
  matrix products: 14.4 us -> 0 us
  between operations: 13.4 us -> 0.04 us
  starting transfers between devices: 6.38 us -> 0 us
  local copies, waits for them, and re-layouts: 7.89 us -> 4.39 us
    all_to_all x1 -> x0, blocking collectives: 190 us -> none  [local(): lax.all_to_all(outgoing, 'pool', split_axis=0, concat_axis=0, tiled=True)]
    pallas_call x0 -> x1, Pallas kernels: none -> 119 us  [split_depth(): pl.pallas_call(functools.partial(kernel, group, reps, parts), out_shape=j...]
    all_to_all x1 -> x0, waiting for transfers between devices: 14.5 us -> none  [local(): lax.all_to_all(expanded.reshape(devices, capacity, out_width), 'pool', sp...]
    dot_general x2 -> x0, matrix products: 14.4 us -> none  [the longest x1 9.45 us: local(): jnp.dot(tokens, lax.all_gather(key_projection_weight, 'pool', axis=0, til...]
    scatter x1 -> x0, local copies, waits for them, and re-layouts: 7.02 us -> none  [local(): jnp.zeros((devices * capacity, width), jnp.bfloat16).at[slot_index]]
    all_to_all x1 -> x0, starting transfers between devices: 6.38 us -> none  [local(): lax.all_to_all(expanded.reshape(devices, capacity, out_width), 'pool', sp...]
    unnamed x4 -> x8, local copies, waits for them, and re-layouts: 0.01 us -> 4.39 us
  transfers between devices with their start and end apart: 2 -> 0, of which waited for: 1 -> 0; matrix products, arithmetic and copies ran while one was open for 6% -> 0% of each run, Pallas kernels for 0% -> 0%
where the time goes in v1:
time: 125 us; the launch traced here: 124 us
  Pallas kernels  119 us (95%)
  local copies, waits for them, and re-layouts  4.39 us (4%)
    pallas_call x1, Pallas kernels, split_depth(): pl.pallas_call(functools.partial(kernel, group, reps, parts), out_shape=j...  119 us
    unnamed x8, local copies, waits for them, and re-layouts  4.39 us

profile of v1, /device:TPU:0, one launch (start us, length us, event | category | flops | bytes accessed | tf_op | source)
XLA Modules:
  0.0 124.1 jit_solution(5579122712934974875)
XLA Ops:
  0.0 0.0 copy-start.2
  0.0 0.0 copy-start.1
  0.0 0.8 convert_bitcast_fusion
  0.8 2.1 %copy.6 = bf16[1,8192,64]{2,1,0:T(8,128)(2,1)S(1)} copy(bf16[1,8192,64]{1,2,0:T(8,128)(2,1)} %param.7) | data formatting | bytes 2097152 | tf_op args[2]
  2.9 0.0 copy-done.2
  2.9 0.0 copy-done.1
  2.9 0.0 copy-start
  2.9 1.6 %copy-done = bf16[128,8192]{1,0:T(8,128)(2,1)S(1)} copy-done((bf16[128,8192]{1,0:T(8,128)(2,1)S(1)}, bf16[128,8192]{1,0:T(8,128)(2,1)}, u32[]{:S(2)}) %copy-start) | copy-done | bytes 2097176
  4.5 118.9 %shard_map.55 = bf16[128,1024]{1,0:T(8,128)(2,1)S(1)} custom-call(bf16[128,8192]{1,0:T(8,128)(2,1)S(1)} %copy-done, bf16[512,1024]{1,0:T(8,128)(2,1)S(1)} %copy-done.1, bf16[8192,64]{1,0:T(8,128)(2,1)S(1)} %bitcast.4, bf16[64,1024]{1,0:T(8,128)(2,1)S(1)} %bitcast.5, f32[8,128]{1,0:T(8,128)S(1)} %broadcast_in_dim.8.id_ref), custom_call_target="tpu_custom_call" | custom-call | tf_op jit(solution)/shard_map/pallas_call | solution.py:227
  123.4 0.7 copy.8
  (1 shorter events, 0.0 us)
Async XLA Ops:
  0.0 2.9 %copy-start.2 = (bf16[1,64,1024]{2,1,0:T(8,128)(2,1)S(1)}, bf16[1,64,1024]{2,1,0:T(8,128)(2,1)}, u32[]{:S(2)}) copy-start(bf16[1,64,1024]{2,1,0:T(8,128)(2,1)} %param.8) | copy-start | bytes 393220
  0.0 2.9 %copy-start.1 = (bf16[512,1024]{1,0:T(8,128)(2,1)S(1)}, bf16[512,1024]{1,0:T(8,128)(2,1)}, u32[]{:S(2)}) copy-start(bf16[512,1024]{1,0:T(8,128)(2,1)} %w_hbm.1) | copy-start | bytes 3145732
  2.9 1.6 %copy-start = (bf16[128,8192]{1,0:T(8,128)(2,1)S(1)}, bf16[128,8192]{1,0:T(8,128)(2,1)}, u32[]{:S(2)}) copy-start(bf16[128,8192]{1,0:T(8,128)(2,1)} %x_hbm.1) | copy-start | bytes 6291460

commit v2 on v1

v2 whole, which is shorter than its diff:
```python
import functools

import jax
import jax.numpy as jnp
from jax import lax
from jax.experimental import pallas as pl
from jax.experimental.pallas import tpu as pltpu
from jax.sharding import PartitionSpec as P

HALVES = 2
CORES = 2
W_FIRST = False
LANES = 128
MESH = pl.DeviceIdType.MESH


def kernel(
    group, reps, parts,
    x_hbm, w_hbm, a_hbm, b_hbm, id_ref, out_ref,
    xr, ar, wf, bp, idr, slots, acc, base, srecv, s2, s2m, cpart, pair, cpair, crecv,
    x_send, x_recv, a_send, a_recv, w_send, w_recv, f_send, f_recv, b_send, b_recv,
    i_send, i_recv, s_send, s_recv, t_send, t_recv, p_send, p_recv, c_send, c_recv, local_sem,
):
    rep = lax.axis_index("rep")
    pool = lax.axis_index("pool")
    half, e = pool // group, pool % group
    rows, out_width = out_ref.shape
    depth = w_hbm.shape[0]
    low = group * depth
    rank = b_hbm.shape[0]
    devices = group * HALVES
    part = out_width // parts
    partner = (pool + group) % devices
    sides = group // CORES
    core = e % CORES
    core_peer = half * group + e + 1 - 2 * core

    def peer(k):
        return half * group + (e + k) % group

    def place(i):
        return (i % CORES) * sides + i // CORES

    def row_at(i, count=1):
        return pl.ds(pl.multiple_of(i * rows, rows), count * rows)

    def col_at(i, size):
        return pl.ds(pl.multiple_of(i * size, size), size)

    def depth_at(b, i):
        return pl.ds(pl.multiple_of(b * low + i * depth, depth), depth)

    def remote(src, dst, send, recv, device):
        return pltpu.make_async_remote_copy(
            src_ref=src, dst_ref=dst, send_sem=send, recv_sem=recv,
            device_id=device, device_id_type=MESH,
        )

    barrier = pltpu.get_barrier_semaphore()
    for k in range(1, devices):
        pl.semaphore_signal(
            barrier, inc=1, device_id={"pool": (pool + k) % devices}, device_id_type=MESH
        )
    for k in range(1, reps):
        pl.semaphore_signal(
            barrier, inc=1, device_id={"rep": (rep + k) % reps}, device_id_type=MESH
        )

    my_place = place(e)
    my_rows = row_at(my_place)
    slot = e * HALVES + half
    my_slot = pl.ds(pl.multiple_of(slot * rank, rank), rank)
    own_b = pl.ds(pl.multiple_of(half * rank, rank), rank)
    own = [
        pltpu.make_async_copy(w_hbm, wf.at[half], local_sem.at[0]),
        pltpu.make_async_copy(b_hbm, bp.at[own_b], local_sem.at[1]),
    ]
    for b in range(HALVES):
        own.append(pltpu.make_async_copy(
            x_hbm.at[:, depth_at(b, e)], xr.at[b, my_rows], local_sem.at[2 + 2 * b]
        ))
        own.append(pltpu.make_async_copy(
            a_hbm.at[:, depth_at(b, e)], ar.at[b, my_slot], local_sem.at[3 + 2 * b]
        ))
    for copy in own:
        copy.start()
    idr[my_place] = id_ref[...]
    pl.semaphore_wait(barrier, devices - 1 + reps - 1)

    sends, x_copies, a_copies = [], [], []

    def launch(copy):
        copy.start()
        sends.append(copy)
        return copy

    def send_a(n, device):
        for b in range(HALVES):
            a_copies.append(launch(remote(
                a_hbm.at[:, depth_at(b, device % group)], ar.at[b, my_slot],
                a_send.at[b, n], a_recv.at[b, n], {"pool": device},
            )))

    share = parts // reps
    w_copies = []

    def send_w():
        for n in range(share):
            at = col_at(n * reps + rep, part)
            w_copies.append(launch(remote(
                w_hbm.at[:, at], wf.at[half, :, at], w_send.at[n], w_recv.at[n],
                {"pool": partner},
            )))

    if W_FIRST:
        send_w()
    for k in range(1, group):
        x_copies.append(launch(remote(
            id_ref, idr.at[my_place], i_send.at[k], i_recv.at[k], {"pool": peer(k)}
        )))
    for k in range(1, group):
        for b in range(HALVES):
            x_copies.append(launch(remote(
                x_hbm.at[:, depth_at(b, (e + k) % group)], xr.at[b, my_rows],
                x_send.at[b, k], x_recv.at[b, k], {"pool": peer(k)},
            )))
        send_a(group + k, (1 - half) * group + (e + k) % group)
        send_a(k, peer(k))
    send_a(group, partner)
    if not W_FIRST:
        send_w()
    b_copy = launch(remote(b_hbm, bp.at[own_b], b_send, b_recv, {"pool": partner}))

    for copy in x_copies:
        copy.wait_recv()
    for copy in own:
        copy.wait()

    lane = lax.broadcasted_iota(jnp.int32, (rows, LANES), 1)
    eye = lane == lax.broadcasted_iota(jnp.int32, (rows, LANES), 0)
    upper = jnp.where(lane >= rank, 1.0, 0.0)

    @pl.loop(0, group)
    def _(i):
        line = jnp.broadcast_to(idr[i], (rows, LANES)).astype(jnp.float32)
        column = jnp.sum(jnp.where(eye, line, 0.0), axis=1, keepdims=True)
        column = jnp.where(
            column >= float(group), HALVES * (column - float(group)) + 1.0, HALVES * column
        )
        slots[row_at(i)] = jnp.broadcast_to(column, (rows, LANES)) - upper

    @pl.loop(0, parts)
    def _(j):
        at = col_at(j, part)
        base[:, at] = jnp.dot(
            xr[half], wf[half, :, at], preferred_element_type=jnp.float32
        )

    def forward_w():
        copies = []
        for n in range(share):
            w_copies[n].wait_recv()
            piece = wf.at[1 - half, :, col_at(n * reps + rep, part)]
            copies.append(launch(remote(
                piece, piece, f_send.at[n], f_recv.at[n], {"rep": (rep + 1) % reps}
            )))
        return copies

    if W_FIRST:
        f_copies = forward_w()
    for copy in a_copies:
        copy.wait_recv()
    acc[...] = jnp.zeros_like(acc)
    wide = 4 * rank

    @pl.loop(0, devices * rank // wide)
    def _(j):
        at = pl.ds(pl.multiple_of(j * wide, wide), wide)
        t = jnp.zeros((group * rows, wide), jnp.float32)
        for b in range(HALVES):
            t += lax.dot_general(
                xr[b], ar[b, at], (((1,), (1,)), ((), ())),
                preferred_element_type=jnp.float32,
            )
        first = (4 * j).astype(jnp.float32)
        acc[...] = jnp.where(
            slots[...] == first, t[:, :LANES],
            jnp.where(slots[...] == first + 2.0, t[:, LANES:], acc[...]),
        )

    s_copies = []
    for k in range(1, group):
        s_copies.append(launch(remote(
            acc.at[row_at(place((e + k) % group))], srecv.at[k], s_send.at[k], s_recv.at[k],
            {"pool": peer(k)},
        )))
    if not W_FIRST:
        f_copies = forward_w()
    total = acc[my_rows]
    for k in range(1, group):
        s_copies[k - 1].wait_recv()
        total += srecv[k]
    s2[my_rows] = total.astype(jnp.bfloat16)
    t_copies = []
    for k in range(1, group):
        t_copies.append(launch(remote(
            s2.at[my_rows], s2.at[my_rows], t_send.at[k], t_recv.at[k], {"pool": peer(k)}
        )))

    for n in range(share):
        f_copies[n].wait_recv()

    @pl.loop(0, parts)
    def _(j):
        at = col_at(j, part)
        base[:, at] += jnp.dot(
            xr[1 - half], wf[1 - half, :, at], preferred_element_type=jnp.float32
        )

    for copy in t_copies:
        copy.wait_recv()
    b_copy.wait_recv()
    mine = (HALVES * e).astype(jnp.float32)
    s2m[...] = jnp.where(
        slots[...] == mine, s2[...].astype(jnp.float32), 0.0
    ).astype(jnp.bfloat16)

    here, there = row_at(core * sides, sides), row_at((1 - core) * sides, sides)
    p_copies, c_copies = [], []

    def pair_up(j):
        at = pl.ds(j * part, part)
        update = jnp.dot(s2m[...], bp[:, at], preferred_element_type=jnp.float32)
        update = update.astype(jnp.bfloat16).astype(jnp.float32)
        base[:, at] += 2.0 * update
        cpart[:, at] = base[there, at].astype(jnp.bfloat16)
        p_copies.append(launch(remote(
            cpart.at[:, at], pair.at[:, at], p_send.at[j], p_recv.at[j], {"pool": core_peer}
        )))

    def hand_on(j):
        at = pl.ds(j * part, part)
        p_copies[j].wait_recv()
        cpair[:, at] = (base[here, at] + pair[:, at].astype(jnp.float32)).astype(jnp.bfloat16)
        for k in range(1, sides):
            to = (e // CORES + k) % sides
            c_copies.append(launch(remote(
                cpair.at[row_at(to), at], crecv.at[k, :, at], c_send.at[j, k], c_recv.at[j, k],
                {"pool": half * group + to * CORES + core},
            )))

    for j in range(parts):
        pair_up(j)
        if j > 0:
            hand_on(j - 1)
    hand_on(parts - 1)
    for j in range(parts):
        at = pl.ds(j * part, part)
        value = cpair[row_at(e // CORES), at].astype(jnp.float32)
        for k in range(1, sides):
            c_copies[j * (sides - 1) + k - 1].wait_recv()
            value += crecv[k, :, at].astype(jnp.float32)
        out_ref[:, at] = value.astype(jnp.bfloat16)
    for copy in sends:
        copy.wait_send()


def split_depth(
    tokens, key_projection_weight, adapter_down_factors, adapter_up_factors, request_adapter_index
):
    rows = tokens.shape[0]
    depth, out_width = key_projection_weight.shape
    rank = adapter_down_factors.shape[2]
    devices = lax.axis_size("pool")
    reps = lax.axis_size("rep")
    group = devices // HALVES
    sides = group // CORES
    parts = 2 * reps
    everyone = group * rows
    ids = request_adapter_index.reshape(1, rows)
    bf16, f32 = jnp.bfloat16, jnp.float32
    dma = pltpu.SemaphoreType.DMA
    hbm, vmem = pl.BlockSpec(memory_space=pl.ANY), pl.BlockSpec(memory_space=pltpu.VMEM)
    return pl.pallas_call(
        functools.partial(kernel, group, reps, parts),
        out_shape=jax.ShapeDtypeStruct((rows, out_width), bf16),
        in_specs=[hbm, hbm, hbm, hbm, vmem],
        out_specs=vmem,
        scratch_shapes=[
            pltpu.VMEM((HALVES, everyone, depth), bf16),
            pltpu.VMEM((HALVES, devices * rank, depth), bf16),
            pltpu.VMEM((HALVES, depth, out_width), bf16),
            pltpu.VMEM((HALVES * rank, out_width), bf16),
            pltpu.VMEM((group, 1, rows), jnp.int32),
            pltpu.VMEM((everyone, LANES), f32),
            pltpu.VMEM((everyone, LANES), f32),
            pltpu.VMEM((everyone, out_width), f32),
            pltpu.VMEM((group, rows, LANES), f32),
            pltpu.VMEM((everyone, LANES), bf16),
            pltpu.VMEM((everyone, LANES), bf16),
            pltpu.VMEM((sides * rows, out_width), bf16),
            pltpu.VMEM((sides * rows, out_width), bf16),
            pltpu.VMEM((sides * rows, out_width), bf16),
            pltpu.VMEM((sides, rows, out_width), bf16),
            dma((HALVES, group)), dma((HALVES, group)),
            dma((HALVES, devices)), dma((HALVES, devices)),
            dma((parts,)), dma((parts,)),
            dma((parts,)), dma((parts,)),
            dma, dma,
            dma((group,)), dma((group,)),
            dma((group,)), dma((group,)),
            dma((group,)), dma((group,)),
            dma((parts,)), dma((parts,)),
            dma((parts, sides)), dma((parts, sides)),
            dma((6,)),
        ],
        compiler_params=pltpu.CompilerParams(
            collective_id=0, has_side_effects=True, vmem_limit_bytes=60 << 20
        ),
    )(
        tokens, key_projection_weight, jnp.swapaxes(adapter_down_factors, 1, 2)[0],
        adapter_up_factors[0], ids,
    )


def route_rows(
    tokens, key_projection_weight, adapter_down_factors, adapter_up_factors, request_adapter_index
):
    row_count = tokens.shape[0]
    width = tokens.shape[1]
    devices = lax.axis_size("pool")
    rows_by_device = adapter_down_factors.shape[0]
    out_width = key_projection_weight.shape[1]
    per_adapter = max(2, 2 * row_count // (rows_by_device * devices))
    capacity = rows_by_device * per_adapter
    adapter_col = request_adapter_index[:, 0]
    same = adapter_col[:, None] == adapter_col[None, :]
    positions = jnp.arange(row_count, dtype=jnp.int32)
    earlier = positions[None, :] < positions[:, None]
    rank_within = jnp.sum((same & earlier).astype(jnp.int32), axis=1)
    slot_index = adapter_col * per_adapter + rank_within
    base = jnp.dot(
        tokens,
        lax.all_gather(key_projection_weight, "pool", axis=0, tiled=True),
        preferred_element_type=jnp.float32,
    )
    outgoing = jnp.zeros((devices * capacity, width), jnp.bfloat16).at[slot_index].set(tokens)
    outgoing = outgoing.reshape(devices, capacity, width)
    received_rows = lax.all_to_all(outgoing, "pool", split_axis=0, concat_axis=0, tiled=True)
    received_rows = received_rows.reshape(devices, rows_by_device, per_adapter, width)
    rank_reduced = jnp.einsum(
        "qhey,hyt->qhet", received_rows, adapter_down_factors, preferred_element_type=jnp.float32
    ).astype(jnp.bfloat16)
    expanded = jnp.einsum(
        "zydk,ykj->zydj", rank_reduced, adapter_up_factors, preferred_element_type=jnp.float32
    ).astype(jnp.bfloat16)
    returned = lax.all_to_all(
        expanded.reshape(devices, capacity, out_width),
        "pool",
        split_axis=0,
        concat_axis=0,
        tiled=True,
    )
    delta = returned.reshape(devices * capacity, out_width)[slot_index]
    return (base + 2.0 * delta.astype(jnp.float32)).astype(jnp.bfloat16)


def local(
    tokens, key_projection_weight, adapter_down_factors, adapter_up_factors, request_adapter_index
):
    fits = (
        key_projection_weight.shape[0] % LANES == 0
        and tokens.shape[0] == LANES
        and adapter_down_factors.shape[0] == 1
        and HALVES * adapter_down_factors.shape[2] == LANES
        and lax.axis_size("pool") % (HALVES * CORES) == 0
        and lax.axis_size("rep") == 2
    )
    plan = split_depth if fits else route_rows
    return plan(
        tokens, key_projection_weight, adapter_down_factors, adapter_up_factors,
        request_adapter_index,
    )


def solution(mesh):
    in_specs = (
        P(("rep", "pool"), None),
        P("pool", None),
        P(("rep", "pool"), None, None),
        P(("rep", "pool"), None, None),
        P(("rep", "pool"), None),
    )
    out_specs = P(("rep", "pool"), None)
    return jax.shard_map(local, mesh=mesh, in_specs=in_specs, out_specs=out_specs, check_vma=False)
```

time: 125 us -> 109 us (0.87)
  Pallas kernels: 119 us -> 107 us
  local copies, waits for them, and re-layouts: 4.39 us -> 1.67 us
    pallas_call x1, Pallas kernels: 119 us -> 107 us  [split_depth(): pl.pallas_call(functools.partial(kernel, group, reps, parts), out_shape=j...]
    unnamed x8 -> x1, local copies, waits for them, and re-layouts: 4.39 us -> 1.67 us
where the time goes in v2:
time: 109 us
  Pallas kernels  107 us (98%)
  local copies, waits for them, and re-layouts  1.67 us (2%)
    pallas_call x1, Pallas kernels, split_depth(): pl.pallas_call(functools.partial(kernel, group, reps, parts), out_shape=j...  107 us

profile of v2, /device:TPU:0, one launch (start us, length us, event | category | flops | bytes accessed | tf_op | source)
XLA Modules:
  0.0 108.7 jit_solution(4601047299815599464)
XLA Ops:
  0.0 107.0 %shard_map.55 = bf16[128,1024]{1,0:T(8,128)(2,1)} custom-call(bf16[128,8192]{1,0:T(8,128)(2,1)} %x_hbm.1, bf16[512,1024]{1,0:T(8,128)(2,1)} %w_hbm.1, bf16[64,8192]{1,0:T(8,128)(2,1)} %bitcast.5, bf16[64,1024]{1,0:T(8,128)(2,1)} %bitcast.6, s32[1,128]{1,0:T(1,128)} %bitcast.7), custom_call_target="tpu_custom_call" | custom-call | tf_op jit(solution)/shard_map/pallas_call | solution.py:284
  107.0 1.7 %copy.7 = bf16[128,1024]{1,0:T(8,128)(2,1)} copy(bf16[128,1024]{1,0:T(8,128)(2,1)} %shard_map.55) | data formatting | bytes 524288

commit v3 on v2

--- a/solution.py
+++ b/solution.py
@@ -17,7 +17,7 @@
 def kernel(
     group, reps, parts,
     x_hbm, w_hbm, a_hbm, b_hbm, id_ref, out_ref,
-    xr, ar, wf, bp, idr, slots, acc, base, srecv, s2, s2m, cpart, pair, cpair, crecv,
+    xr, ar, wf, bp, idr, slots, acc, base, sp, srecv, s2, s2m, cpart, pair, cpair, crecv,
     x_send, x_recv, a_send, a_recv, w_send, w_recv, f_send, f_recv, b_send, b_recv,
     i_send, i_recv, s_send, s_recv, t_send, t_recv, p_send, p_recv, c_send, c_recv, local_sem,
 ):
@@ -188,10 +188,11 @@
             jnp.where(slots[...] == first + 2.0, t[:, LANES:], acc[...]),
         )
 
+    sp[...] = acc[...].astype(jnp.bfloat16)
     s_copies = []
     for k in range(1, group):
         s_copies.append(launch(remote(
-            acc.at[row_at(place((e + k) % group))], srecv.at[k], s_send.at[k], s_recv.at[k],
+            sp.at[row_at(place((e + k) % group))], srecv.at[k], s_send.at[k], s_recv.at[k],
             {"pool": peer(k)},
         )))
     if not W_FIRST:
@@ -199,7 +200,7 @@
     total = acc[my_rows]
     for k in range(1, group):
         s_copies[k - 1].wait_recv()
-        total += srecv[k]
+        total += srecv[k].astype(jnp.float32)
     s2[my_rows] = total.astype(jnp.bfloat16)
     t_copies = []
     for k in range(1, group):
@@ -295,7 +296,8 @@
             pltpu.VMEM((everyone, LANES), f32),
             pltpu.VMEM((everyone, LANES), f32),
             pltpu.VMEM((everyone, out_width), f32),
-            pltpu.VMEM((group, rows, LANES), f32),
+            pltpu.VMEM((everyone, LANES), bf16),
+            pltpu.VMEM((group, rows, LANES), bf16),
             pltpu.VMEM((everyone, LANES), bf16),
             pltpu.VMEM((everyone, LANES), bf16),
             pltpu.VMEM((sides * rows, out_width), bf16),

time: 109 us -> 108 us (level)
  no operation moved by 1% of the time
where the time goes in v3:
time: 108 us
  Pallas kernels  106 us (98%)
  local copies, waits for them, and re-layouts  1.67 us (2%)
    pallas_call x1, Pallas kernels, split_depth(): pl.pallas_call(functools.partial(kernel, group, reps, parts), out_shape=j...  106 us

profile of v3, /device:TPU:0, one launch (start us, length us, event | category | flops | bytes accessed | tf_op | source)
XLA Modules:
  0.0 108.1 jit_solution(10618933147919410205)
XLA Ops:
  0.0 106.4 %shard_map.55 = bf16[128,1024]{1,0:T(8,128)(2,1)} custom-call(bf16[128,8192]{1,0:T(8,128)(2,1)} %x_hbm.1, bf16[512,1024]{1,0:T(8,128)(2,1)} %w_hbm.1, bf16[64,8192]{1,0:T(8,128)(2,1)} %bitcast.5, bf16[64,1024]{1,0:T(8,128)(2,1)} %bitcast.6, s32[1,128]{1,0:T(1,128)} %bitcast.7), custom_call_target="tpu_custom_call" | custom-call | tf_op jit(solution)/shard_map/pallas_call | solution.py:285
  106.4 1.7 %copy.7 = bf16[128,1024]{1,0:T(8,128)(2,1)} copy(bf16[128,1024]{1,0:T(8,128)(2,1)} %shard_map.55) | data formatting | bytes 524288
